TPU v7x, 512 devices: a whole 4x8x8 slice. The times are simulated.
512 devices in a mesh: row: 16 (over y, core), col: 32 (over x, z).
Axes of the slice: x: 4, y: 8, z: 8, core: 2. Of those that a mesh axis runs over, the one named last changes fastest.
Arguments:
- lam: float32 [14400, 2400], P('row', 'col'), may hold values from -6 to 6
- cycle: float32 [2400, 24000], P('row', 'col'), may hold values from -0.125 to 0.125
- eps_occ: float32 [200], replicated, may hold values from -2 to -0.3
- eps_vir: float32 [1200], replicated, may hold values from 0.1 to 3
- occ_irrep: int32 [200], replicated, may hold values from 0 to 7
- slab: int32 [12], replicated, may hold values from 0 to 199, as said below
- pair_occ: int32 [20], replicated, may hold values from 0 to 199, as said below
- irrep_start: int32 [8], replicated, may hold values from 0 to 1125, as said below
Outputs:
- update: float32 [14400, 24000], P('row', 'col')
Inputs may be any that keep to these rules, and one draw needn't show every extreme that they name: `irrep_start`: entry 0 is 0 and the entries rise strictly, so each irrep holds one or more virtual orbitals; the last entry is 1125; sizes may differ. `slab`: distinct occupied orbitals. `pair_occ`: distinct occupied orbitals.
All inputs are finite; a program needn't handle non-finite values.
Results may differ from a plain program's by a relative error of at most 0.000073.
Values sent between devices are 32-bit elements; how exact they have to be, the bound alone decides.
A program may use at most 128 MiB of HBM per device.

v0:
```python
import jax
import jax.numpy as jnp
from jax import lax
from jax.sharding import PartitionSpec as P

V = 1200


def irrep_of(index, starts):
    return jnp.sum((index[:, None] >= starts[None, :]).astype(jnp.int32), axis=1) - 1


def local(lam, cycle, eps_occ, eps_vir, occ_irrep, slab, pair_occ, irrep_start):
    row_count = lam.shape[0]
    col_count = cycle.shape[1]
    cycle_full = lax.all_gather(cycle, "row", axis=0, tiled=True)
    prod = jnp.dot(
        lax.all_gather(lam, "col", axis=1, tiled=True),
        cycle_full,
        precision=lax.Precision.HIGHEST,
        preferred_element_type=jnp.float32,
    )
    rows = lax.axis_index("row") * row_count + jnp.arange(row_count, dtype=jnp.int32)
    cols = lax.axis_index("col") * col_count + jnp.arange(col_count, dtype=jnp.int32)
    occ_row = jnp.take(slab, rows // V)
    vir_row = rows % V
    occ_col = jnp.take(pair_occ, cols // V)
    vir_col = cols % V
    row_energy = jnp.take(eps_occ, occ_row) - jnp.take(eps_vir, vir_row)
    col_energy = jnp.take(eps_occ, occ_col) - jnp.take(eps_vir, vir_col)
    row_sym = jnp.bitwise_xor(jnp.take(occ_irrep, occ_row), irrep_of(vir_row, irrep_start))
    col_sym = jnp.bitwise_xor(jnp.take(occ_irrep, occ_col), irrep_of(vir_col, irrep_start))
    allowed = row_sym[:, None] == col_sym[None, :]
    denom = row_energy[:, None] + col_energy[None, :]
    return jnp.where(allowed, prod / denom, jnp.float32(0.0))


def solution(mesh):
    placed = (P("row", "col"), P("row", "col"), P(), P(), P(), P(), P(), P())
    return jax.shard_map(
        local, mesh=mesh, in_specs=placed, out_specs=P("row", "col"), check_vma=False
    )
```

profile of v0, /device:TPU:1, one launch (start us, length us, event | category | flops | bytes accessed | tf_op | source)
XLA Modules:
  0.0 253.9 jit_solution(11986677601947028953)
XLA Ops:
  6.5 0.7 all-gather.7.cloned.1.call-update
  7.3 0.7 all-gather.5.cloned.1.call-update
  8.0 1.3 slice.33
  9.4 0.1 compare_reduce_fusion.9
  9.5 0.1 compare_reduce_fusion.11
  9.5 0.1 compare_reduce_fusion.13
  9.6 0.1 compare_reduce_fusion.15
  9.6 2.1 fusion.16
  11.7 4.4 %fusion.11 = (s32[750]{0:T(1024)S(1)}, s32[750]{0:T(1024)S(1)}) fusion(s32[]{:T(128)} %bitcast.28, s32[]{:T(128)} %bitcast.29, s32[]{:T(128)} %bitcast.30, s32[]{:T(128)} %bitcast.31, s32[]{:T(128)} %bitcast.32, s32[]{:T(128)} %bitcast.34, s32[]{:T(128)} %bitcast.33, s32[]{:T(128)S(6)} %mul.7), kind=kLoop, calls=%fused_computation.89 | loop fusion | flops 23250 | bytes 6032 | tf_op jit(solution)/shard_map/jit(_take)/gather | solution.py:27
  16.2 8.2 %select_select_fusion = s32[750]{0:T(1024)S(1)} fusion(pred[750]{0:T(1024)(128)(4,1)S(1)} %get-tuple-element.36, pred[750]{0:T(1024)(128)(4,1)S(1)} %get-tuple-element.37, pred[750]{0:T(1024)(128)(4,1)S(1)} %get-tuple-element.38, pred[750]{0:T(1024)(128)(4,1)S(1)} %get-tuple-element.39, pred[750]{0:T(1024)(128)(4,1)S(1)} %get-tuple-element.40, ...), kind=kLoop, calls=%fused_computation.65 | loop fusion | flops 9750 | bytes 15802 | tf_op jit(solution)/shard_map/jit(_take)/gather | solution.py:27
  24.4 4.8 %gather_fusion.4 = f32[750]{0:T(1024)S(1)} fusion(f32[200]{0:T(256)} %param.10, s32[1024]{0:T(1024)S(1)} %pad_clamp_fusion.2), kind=kCustom, calls=%fused_computation.4 | custom fusion | bytes 9000 | tf_op jit(solution)/shard_map/jit(_take)/gather | solution.py:30
  29.2 0.1 compare_reduce_fusion
  29.3 0.1 compare_reduce_fusion.1
  29.3 0.1 compare_reduce_fusion.2
  29.4 0.1 compare_reduce_fusion.3
  29.4 0.1 compare_reduce_fusion.4
  29.5 1.8 fusion.15
  31.3 4.5 %compare_select_fusion.6 = s32[900,1]{0,1:T(1,128)S(1)} fusion(s32[]{:T(128)} %bitcast.5, s32[]{:T(128)} %bitcast.6, s32[]{:T(128)} %bitcast.7, s32[]{:T(128)} %bitcast.8, s32[]{:T(128)} %bitcast.9, s32[]{:T(128)} %bitcast.11, s32[]{:T(128)} %bitcast.10, s32[]{:T(128)S(6)} %mul.6), kind=kLoop, calls=%fused_computation.20 | loop fusion | flops 21600 | bytes 3632 | tf_op jit(solution)/shard_map/jit(_take)/gather | solution.py:25
  35.7 3.1 %select_select_fusion.1 = s32[900]{0:T(1024)S(1)} fusion(pred[900]{0:T(1024)(128)(4,1)S(1)} %compare_reduce_fusion, pred[900]{0:T(1024)(128)(4,1)S(1)} %compare_reduce_fusion.1, pred[900]{0:T(1024)(128)(4,1)S(1)} %compare_reduce_fusion.2, pred[900]{0:T(1024)(128)(4,1)S(1)} %compare_reduce_fusion.3, pred[900]{0:T(1024)(128)(4,1)S(1)} %compare_reduce_fusion.4, ...), kind=kLoop, calls=%fused_computation.66 | loop fusion | flops 4500 | bytes 11720 | tf_op jit(solution)/shard_map/jit(_take)/gather | solution.py:25
  38.8 0.1 compare_select_fusion
  38.9 6.5 %gather_fusion.2 = f32[900]{0:T(1024)S(1)} fusion(f32[200]{0:T(256)S(1)} %copy-done.1, s32[1024]{0:T(1024)S(1)} %pad_clamp_fusion.3), kind=kCustom, calls=%fused_computation.2 | custom fusion | bytes 10800 | tf_op jit(solution)/shard_map/jit(_take)/gather | solution.py:29
  45.4 5.0 %gather_fusion.1 = s32[750]{0:T(1024)S(1)} fusion(s32[200]{0:T(256)S(1)} %copy-done.2, s32[1024]{0:T(1024)S(1)} %pad_clamp_fusion.2), kind=kCustom, calls=%fused_computation.1 | custom fusion | bytes 9000 | tf_op jit(solution)/shard_map/jit(_take)/gather | solution.py:32
  50.4 6.5 %gather_fusion = s32[900]{0:T(1024)S(1)} fusion(s32[200]{0:T(256)S(1)} %copy-done.2, s32[1024]{0:T(1024)S(1)} %pad_clamp_fusion.3), kind=kCustom, calls=%fused_computation | custom fusion | bytes 10800 | tf_op jit(solution)/shard_map/jit(_take)/gather | solution.py:31
  56.9 4.5 %gather_fusion.5 = f32[750]{0:T(1024)S(1)} fusion(f32[1200]{0:T(1024)S(1)} %copy-done, s32[1024]{0:T(1024)S(1)} %pad_clamp_fusion), kind=kCustom, calls=%fused_computation.5 | custom fusion | bytes 9000 | tf_op jit(solution)/shard_map/jit(_take)/gather | solution.py:30
  61.4 5.9 %gather_fusion.3 = f32[900]{0:T(1024)S(1)} fusion(f32[1200]{0:T(1024)S(1)} %copy-done, s32[1024]{0:T(1024)S(1)} %pad_clamp_fusion.1), kind=kCustom, calls=%fused_computation.3 | custom fusion | bytes 10800 | tf_op jit(solution)/shard_map/jit(_take)/gather | solution.py:29
  67.3 0.1 convert_reduce_fusion.1
  67.4 0.1 convert_reduce_fusion
  67.6 1.7 all-gather.7.cloned.1.call-done
  69.3 6.8 %reshape.467 = f32[2400,750]{1,0:T(8,128)} reshape(f32[16,150,750]{2,1,0:T(8,128)} %all-gather.7.cloned.1.call-done) | data formatting | bytes 14400000
  76.1 109.9 %all-gather.5.cloned.1.call-done = f32[32,75,900]{2,1,0:T(8,128)} async-done(((f32[1,75,900]{2,1,0:T(8,128)}), f32[32,75,900]{2,1,0:T(8,128)}) %all-gather.5.cloned.1.call-update) | async-done | bytes 8640016 | tf_op jit(solution)/shard_map/all_gather | solution.py:18
  186.0 8.2 %reshape.465 = f32[2400,900]{1,0:T(8,128)} reshape(f32[32,75,900]{2,1,0:T(8,128)} %all-gather.5.cloned.1.call-done) | data formatting | bytes 17280000
  194.3 52.8 %divide_select_fusion = f32[900,750]{1,0:T(8,128)} fusion(f32[2400,900]{1,0:T(8,128)} %reshape.465, f32[2400,750]{1,0:T(8,128)} %reshape.467, f32[750]{0:T(1024)S(1)} %select_subtract_fusion, f32[900]{0:T(1024)S(1)} %select_subtract_fusion.1, s32[750]{0:T(1024)S(1)} %add_xor_fusion, s32[900]{0:T(1024)S(1)} %add_xor_fusion.1), kind=kOutput, calls=%fused_computation.6 | convolution fusion | flops 19442702336 | bytes 18553200 | tf_op jit(solution)/shard_map/dot_general | solution.py:17
  (24 shorter events, 0.4 us)
Async XLA Ops:
  6.5 50.4 %copy-start = (f32[1200]{0:T(1024)S(1)}, f32[1200]{0:T(1024)}, u32[]{:S(2)}) copy-start(f32[1200]{0:T(1024)} %param.11) | copy-start | bytes 14404
  6.5 32.3 %copy-start.1 = (f32[200]{0:T(256)S(1)}, f32[200]{0:T(256)}, u32[]{:S(2)}) copy-start(f32[200]{0:T(256)} %param.10) | copy-start | bytes 2404
  6.5 38.9 %copy-start.2 = (s32[200]{0:T(256)S(1)}, s32[200]{0:T(256)}, u32[]{:S(2)}) copy-start(s32[200]{0:T(256)} %param.12) | copy-start | bytes 2404
  6.5 62.8 %all-gather.7.cloned.1.call-start = ((), (), s32[]{:S(2)}) async-start(), calls=%async_computation.1 | async-start | bytes 7938048 | tf_op jit(solution)/shard_map/all_gather | solution.py:16
  7.3 178.8 %all-gather.5.cloned.1.call-start = ((), (), s32[]{:S(2)}) async-start(), calls=%async_computation | async-start | bytes 10813440 | tf_op jit(solution)/shard_map/all_gather | solution.py:18
  45.4 21.9 %copy-start.3 = (s32[8]{0:T(128)S(1)}, s32[8]{0:T(128)}, u32[]{:S(2)}) copy-start(s32[8]{0:T(128)} %param.15) | copy-start | bytes 100
Sparse Core Ops, SparseCore 0:
  9.5 59.7 all-gather.6
  72.5 113.4 all-gather.4
where the time goes:
time: 254 us
  waiting for transfers between devices  113 us (44%)
  local copies, waits for them, and re-layouts  53.2 us (21%)
  matrix products  52.8 us (21%)
  other arithmetic  21.1 us (8%)
  between operations  13.6 us (5%)
    all_gather x1, waiting for transfers between devices, local(): lax.all_gather(lam, 'col', axis=1, tiled=True)  110 us
    dot_general x1, matrix products, local(): jnp.dot(lax.all_gather(lam, 'col', axis=1, tiled=True), cycle_full, preci...  52.8 us
    unnamed x10, local copies, waits for them, and re-layouts  15 us
    gather x9, other arithmetic, local(): occ_col = jnp.take(pair_occ, cols // V)  12.9 us
    gather x2, local copies, waits for them, and re-layouts, local(): row_energy = jnp.take(eps_occ, occ_row) - jnp.take(eps_vir, vir_row)  12.3 us
    gather x2, local copies, waits for them, and re-layouts, local(): col_energy = jnp.take(eps_occ, occ_col) - jnp.take(eps_vir, vir_col)  9.27 us
    gather x7, other arithmetic, local(): occ_row = jnp.take(slab, rows // V)  7.81 us
    gather x1, local copies, waits for them, and re-layouts, local(): jnp.take(occ_irrep, occ_row)  6.49 us
  transfers between devices with their start and end apart: 2, of which 2 were waited for; matrix products, arithmetic and copies ran while one was open for 26% of the time, Pallas kernels for 0%

commit v1 on v0

--- a/solution.py
+++ b/solution.py
@@ -1,9 +1,19 @@
+import functools
 import jax
 import jax.numpy as jnp
 from jax import lax
 from jax.sharding import PartitionSpec as P
+from jax.lax import all_to_all, axis_size
 
 V = 1200
+
+
+def build_zone_all(packet, across):
+    everything = all_to_all(jnp.stack([packet] * axis_size(across)), across, 0, 0)
+    return jnp.concatenate(everything, 1)
+
+
+name_the_waves = functools.partial(build_zone_all, across="col")
 
 
 def irrep_of(index, starts):
@@ -15,7 +25,7 @@
     col_count = cycle.shape[1]
     cycle_full = lax.all_gather(cycle, "row", axis=0, tiled=True)
     prod = jnp.dot(
-        lax.all_gather(lam, "col", axis=1, tiled=True),
+        name_the_waves(lam),
         cycle_full,
         precision=lax.Precision.HIGHEST,
         preferred_element_type=jnp.float32,

time: 254 us -> 337 us (1.33); the launches traced: 254 us -> 333 us
  waiting for transfers between devices: 113 us -> 174 us
  starting transfers between devices: 0.04 us -> 14 us
    all_to_all x0 -> x1, waiting for transfers between devices: none -> 173 us  [build_zone_all(): all_to_all(jnp.stack([packet] * axis_size(across)), across, 0, 0)]
    all_gather x1 -> x0, waiting for transfers between devices: 110 us -> none  [local(): lax.all_gather(lam, 'col', axis=1, tiled=True)]
    all_to_all x0 -> x1, starting transfers between devices: none -> 14 us  [build_zone_all(): all_to_all(jnp.stack([packet] * axis_size(across)), across, 0, 0)]
    unnamed x10 -> x13, local copies, waits for them, and re-layouts: 15 us -> 6.71 us
    reshape x0 -> x1, local copies, waits for them, and re-layouts: none -> 8.22 us  [build_zone_all(): return jnp.concatenate(everything, 1)]
    another operation x0 -> x1, local copies, waits for them, and re-layouts: none -> 6.15 us  [build_zone_all(): jnp.stack([packet] * axis_size(across))]
  transfers between devices with their start and end apart: 2 -> 2, of which waited for: 2 -> 2; matrix products, arithmetic and copies ran while one was open for 26% -> 19% of each run, Pallas kernels for 0% -> 0%
where the time goes in v1:
time: 337 us; the launch traced here: 333 us
  waiting for transfers between devices  174 us (52%)
  local copies, waits for them, and re-layouts  56.4 us (17%)
  matrix products  52.8 us (16%)
  other arithmetic  21.3 us (6%)
  starting transfers between devices  14 us (4%)
  between operations  13.6 us (4%)
    all_to_all x1, waiting for transfers between devices, build_zone_all(): all_to_all(jnp.stack([packet] * axis_size(across)), across, 0, 0)  173 us
    dot_general x1, matrix products, local(): jnp.dot(name_the_waves(lam), cycle_full, precision=lax.Precision.HIGHEST,...  52.8 us
    all_to_all x1, starting transfers between devices, build_zone_all(): all_to_all(jnp.stack([packet] * axis_size(across)), across, 0, 0)  14 us
    gather x9, other arithmetic, local(): occ_col = jnp.take(pair_occ, cols // V)  13 us
    gather x2, local copies, waits for them, and re-layouts, local(): row_energy = jnp.take(eps_occ, occ_row) - jnp.take(eps_vir, vir_row)  12.3 us
    gather x2, local copies, waits for them, and re-layouts, local(): col_energy = jnp.take(eps_occ, occ_col) - jnp.take(eps_vir, vir_col)  9.45 us
    reshape x1, local copies, waits for them, and re-layouts, build_zone_all(): return jnp.concatenate(everything, 1)  8.22 us
    gather x7, other arithmetic, local(): occ_row = jnp.take(slab, rows // V)  7.91 us
  transfers between devices with their start and end apart: 2, of which 2 were waited for; matrix products, arithmetic and copies ran while one was open for 19% of the time, Pallas kernels for 0%

profile of v1, /device:TPU:1, one launch (start us, length us, event | category | flops | bytes accessed | tf_op | source)
XLA Modules:
  0.0 332.6 jit_solution(18395835799524052855)
XLA Ops:
  6.5 6.2 %stack.2 = f32[32,900,75]{1,2,0:T(8,128)} broadcast(f32[900,75]{0,1:T(8,128)} %param.8), dimensions={1,2} | broadcast | bytes 8910000 | tf_op jit(solution)/shard_map/stack | solution.py:12
  12.7 14.0 %all-to-all-start = ((f32[32,900,75]{1,2,0:T(8,128)}), f32[32,900,75]{1,2,0:T(8,128)}, u32[]{:S(2)}, u32[]{:S(2)}) async-start(f32[32,900,75]{1,2,0:T(8,128)} %stack.2), calls=%async_computation | async-start | bytes 20971520 | tf_op jit(solution)/shard_map/all_to_all | solution.py:12
  26.7 0.7 all-gather.3.cloned.1.call-update
  27.4 0.7 slice.33
  28.2 0.1 compare_reduce_fusion.9
  28.3 0.1 compare_reduce_fusion.11
  28.3 0.1 compare_reduce_fusion.13
  28.5 0.7 fusion.16
  29.2 4.4 %fusion.11 = (s32[750]{0:T(1024)S(1)}, s32[750]{0:T(1024)S(1)}) fusion(s32[]{:T(128)} %bitcast.28, s32[]{:T(128)} %bitcast.29, s32[]{:T(128)} %bitcast.30, s32[]{:T(128)} %bitcast.31, s32[]{:T(128)} %bitcast.32, s32[]{:T(128)} %bitcast.34, s32[]{:T(128)} %bitcast.33, s32[]{:T(128)S(6)} %mul.7), kind=kLoop, calls=%fused_computation.89 | loop fusion | flops 23250 | bytes 6032 | tf_op jit(solution)/shard_map/jit(_take)/gather | solution.py:37
  33.6 8.2 %select_select_fusion = s32[750]{0:T(1024)S(1)} fusion(pred[750]{0:T(1024)(128)(4,1)S(1)} %get-tuple-element.36, pred[750]{0:T(1024)(128)(4,1)S(1)} %get-tuple-element.37, pred[750]{0:T(1024)(128)(4,1)S(1)} %get-tuple-element.38, pred[750]{0:T(1024)(128)(4,1)S(1)} %get-tuple-element.39, pred[750]{0:T(1024)(128)(4,1)S(1)} %get-tuple-element.40, ...), kind=kLoop, calls=%fused_computation.65 | loop fusion | flops 9750 | bytes 15802 | tf_op jit(solution)/shard_map/jit(_take)/gather | solution.py:37
  41.9 5.0 %gather_fusion.4 = f32[750]{0:T(1024)S(1)} fusion(f32[200]{0:T(256)S(1)} %copy-done.1, s32[1024]{0:T(1024)S(1)} %pad_clamp_fusion.2), kind=kCustom, calls=%fused_computation.4 | custom fusion | bytes 9000 | tf_op jit(solution)/shard_map/jit(_take)/gather | solution.py:40
  46.9 0.1 compare_reduce_fusion
  46.9 0.1 compare_reduce_fusion.1
  47.0 0.1 compare_reduce_fusion.2
  47.0 0.1 compare_reduce_fusion.3
  47.1 0.1 compare_reduce_fusion.4
  47.1 0.7 fusion.15
  47.8 4.5 %compare_select_fusion.6 = s32[900,1]{0,1:T(1,128)S(1)} fusion(s32[]{:T(128)} %bitcast.5, s32[]{:T(128)} %bitcast.6, s32[]{:T(128)} %bitcast.7, s32[]{:T(128)} %bitcast.8, s32[]{:T(128)} %bitcast.9, s32[]{:T(128)} %bitcast.11, s32[]{:T(128)} %bitcast.10, s32[]{:T(128)S(6)} %mul.6), kind=kLoop, calls=%fused_computation.20 | loop fusion | flops 21600 | bytes 3632 | tf_op jit(solution)/shard_map/jit(_take)/gather | solution.py:35
  52.3 3.2 select_select_fusion.1
  55.5 0.1 compare_select_fusion
  55.6 6.5 %gather_fusion.2 = f32[900]{0:T(1024)S(1)} fusion(f32[200]{0:T(256)S(1)} %copy-done.1, s32[1024]{0:T(1024)S(1)} %pad_clamp_fusion.3), kind=kCustom, calls=%fused_computation.2 | custom fusion | bytes 10800 | tf_op jit(solution)/shard_map/jit(_take)/gather | solution.py:39
  62.1 5.0 %gather_fusion.1 = s32[750]{0:T(1024)S(1)} fusion(s32[200]{0:T(256)S(1)} %copy-done.2, s32[1024]{0:T(1024)S(1)} %pad_clamp_fusion.2), kind=kCustom, calls=%fused_computation.1 | custom fusion | bytes 9000 | tf_op jit(solution)/shard_map/jit(_take)/gather | solution.py:42
  67.1 6.5 %gather_fusion = s32[900]{0:T(1024)S(1)} fusion(s32[200]{0:T(256)S(1)} %copy-done.2, s32[1024]{0:T(1024)S(1)} %pad_clamp_fusion.3), kind=kCustom, calls=%fused_computation | custom fusion | bytes 10800 | tf_op jit(solution)/shard_map/jit(_take)/gather | solution.py:41
  73.6 4.5 %gather_fusion.5 = f32[750]{0:T(1024)S(1)} fusion(f32[1200]{0:T(1024)S(1)} %copy-done, s32[1024]{0:T(1024)S(1)} %pad_clamp_fusion), kind=kCustom, calls=%fused_computation.5 | custom fusion | bytes 9000 | tf_op jit(solution)/shard_map/jit(_take)/gather | solution.py:40
  78.1 5.9 %gather_fusion.3 = f32[900]{0:T(1024)S(1)} fusion(f32[1200]{0:T(1024)S(1)} %copy-done, s32[1024]{0:T(1024)S(1)} %pad_clamp_fusion.1), kind=kCustom, calls=%fused_computation.3 | custom fusion | bytes 10800 | tf_op jit(solution)/shard_map/jit(_take)/gather | solution.py:39
  84.0 0.1 convert_reduce_fusion.1
  84.1 0.1 convert_reduce_fusion
  84.3 1.2 all-gather.3.cloned.1.call-done
  85.5 6.7 %reshape.475 = f32[2400,750]{1,0:T(8,128)} reshape(f32[16,150,750]{2,1,0:T(8,128)} %all-gather.3.cloned.1.call-done) | data formatting | bytes 14400000
  92.2 172.5 %all-to-all-done = f32[32,900,75]{1,2,0:T(8,128)} async-done(((f32[32,900,75]{1,2,0:T(8,128)}), f32[32,900,75]{1,2,0:T(8,128)}, u32[]{:S(2)}, u32[]{:S(2)}) %all-to-all-start) | async-done | bytes 8640032 | tf_op jit(solution)/shard_map/all_to_all | solution.py:12
  264.7 8.2 %reshape.305 = f32[900,2400]{0,1:T(8,128)} reshape(f32[900,32,75]{0,2,1:T(8,128)} %bitcast.35) | data formatting | bytes 17280000 | tf_op jit(solution)/shard_map/reshape | solution.py:13
  272.9 52.8 %divide_select_fusion = f32[900,750]{1,0:T(8,128)} fusion(f32[900,2400]{0,1:T(8,128)} %reshape.305, f32[2400,750]{1,0:T(8,128)} %reshape.475, f32[750]{0:T(1024)S(1)} %select_subtract_fusion, f32[900]{0:T(1024)S(1)} %select_subtract_fusion.1, s32[750]{0:T(1024)S(1)} %add_xor_fusion, s32[900]{0:T(1024)S(1)} %add_xor_fusion.1), kind=kOutput, calls=%fused_computation.6 | convolution fusion | flops 19442702336 | bytes 18553200 | tf_op jit(solution)/shard_map/dot_general | solution.py:27
  (28 shorter events, 0.5 us)
Async XLA Ops:
  6.5 67.1 %copy-start = (f32[1200]{0:T(1024)S(1)}, f32[1200]{0:T(1024)}, u32[]{:S(2)}) copy-start(f32[1200]{0:T(1024)} %param.11) | copy-start | bytes 14404
  12.7 14.7 %copy-start.3 = (s32[20]{0:T(128)S(1)}, s32[20]{0:T(128)}, u32[]{:S(2)}) copy-start(s32[20]{0:T(128)} %param.14) | copy-start | bytes 244
  12.7 29.2 %copy-start.1 = (f32[200]{0:T(256)S(1)}, f32[200]{0:T(256)}, u32[]{:S(2)}) copy-start(f32[200]{0:T(256)} %param.10) | copy-start | bytes 2404
  12.7 34.5 %copy-start.4 = (s32[12]{0:T(128)S(1)}, s32[12]{0:T(128)}, u32[]{:S(2)}) copy-start(s32[12]{0:T(128)} %param.13) | copy-start | bytes 148
  12.7 252.0 %all-to-all-start = ((f32[32,900,75]{1,2,0:T(8,128)}), f32[32,900,75]{1,2,0:T(8,128)}, u32[]{:S(2)}, u32[]{:S(2)}) async-start(f32[32,900,75]{1,2,0:T(8,128)} %stack.2), calls=%async_computation | async-start | bytes 20971520 | tf_op jit(solution)/shard_map/all_to_all | solution.py:12
  26.7 35.4 %copy-start.2 = (s32[200]{0:T(256)S(1)}, s32[200]{0:T(256)}, u32[]{:S(2)}) copy-start(s32[200]{0:T(256)} %param.12) | copy-start | bytes 2404
  26.7 58.8 %all-gather.3.cloned.1.call-start = ((), (), s32[]{:S(2)}) async-start(), calls=%async_computation.1 | async-start | bytes 7938048 | tf_op jit(solution)/shard_map/all_gather | solution.py:26
  62.1 21.9 %copy-start.5 = (s32[8]{0:T(128)S(1)}, s32[8]{0:T(128)}, u32[]{:S(2)}) copy-start(s32[8]{0:T(128)} %param.15) | copy-start | bytes 100
Sparse Core Ops, SparseCore 0:
  29.6 55.8 all-gather.2
